TPU v7x, 512 devices: a whole 4x4x16 slice. The times are simulated.
512 devices in a mesh: replica: 16 (over x, z_hi, core), fsdp: 32 (over y, z_lo).
Axes of the slice: x: 4, y: 4, z: 16 (z_hi: 2, z_lo: 8; z = z_hi * 8 + z_lo), core: 2. Of those that a mesh axis runs over, the one named last changes fastest.
Arguments:
- tokens: bfloat16 [16, 4096, 8192], P('replica', 'fsdp'), may hold values from -6 to 6
- norm_gain: bfloat16 [8192], replicated, may hold values from 0.099609375 to 1.8984375
- cotangent: bfloat16 [16, 4096, 1024], P('replica', 'fsdp'), may hold values from -6 to 6
- layer_weight: bfloat16 [16, 8192, 1024], P('replica', 'fsdp'), may hold values from -0.09375 to 0.09375
- shared_copy: bfloat16 [8192, 1024], P('fsdp'), may hold values from -0.0625 to 0.0625
- master: float32 [8192, 1024], P('fsdp', 'replica'), may hold values from -0.0625 to 0.0625
- momentum: float32 [8192, 1024], P('fsdp', 'replica'), may hold values from -0.078125 to 0.078125
Outputs:
- layer_next: bfloat16 [16, 8192, 1024], P('replica', 'fsdp')
- master_next: float32 [8192, 1024], P('fsdp', 'replica')
- momentum_next: float32 [8192, 1024], P('fsdp', 'replica')
All inputs are finite; a program needn't handle non-finite values.
Results may differ from a plain program's by a relative error of at most 0.013.
Values may be sent and summed in bfloat16 or wider, within the bound.
A program may use at most 64 MiB of HBM per device.

v0:
```python
import math

import jax
import jax.numpy as jnp
from jax import lax
from jax.sharding import PartitionSpec as P

BLOCK = 64


norm_eps = 1e-05
inner_gain = 0.4
outer_rate = 0.7
outer_beta = 0.9
mix_weight = 0.5
code_range = 448.0


def on_device(tokens, norm_gain, cotangent, layer_weight, shared_copy, master, momentum):
    tok_float = tokens[0].astype(jnp.float32)
    inverse = lax.rsqrt(jnp.mean(tok_float * tok_float, axis=-1, keepdims=True) + norm_eps)
    normed = (tok_float * inverse * norm_gain.astype(jnp.float32)).astype(jnp.bfloat16)
    columns = lax.all_to_all(normed, "fsdp", split_axis=1, concat_axis=0, tiled=True)
    local_rows = columns.shape[1]
    width = cotangent.shape[2]
    inner_rate = inner_gain / math.sqrt(columns.shape[0])
    grad = lax.dot_general(
        columns,
        lax.all_gather(cotangent[0], "fsdp", axis=0, tiled=True),
        (((0,), (0,)), ((), ())),
        preferred_element_type=jnp.float32,
    )
    weight_float = layer_weight[0].astype(jnp.float32)
    delta = (shared_copy.astype(jnp.float32) - weight_float).reshape(
        local_rows, width // BLOCK, BLOCK
    )
    largest = jnp.max(jnp.abs(delta), axis=-1, keepdims=True)
    scale = ((largest + 1e-06) / code_range).astype(jnp.bfloat16)
    coded = (delta / scale.astype(jnp.float32)).astype(jnp.bfloat16)
    groups = lax.axis_size("replica")
    share = width // BLOCK // groups
    decoded = lax.optimization_barrier(coded).astype(jnp.float32) * scale.astype(jnp.float32)
    owned = lax.psum_scatter(
        decoded.astype(jnp.bfloat16), "replica", scatter_dimension=1, tiled=True
    ).astype(jnp.float32)
    average = owned.reshape(local_rows, share * BLOCK) / groups
    momentum_next = outer_beta * momentum + average
    master_next = master - outer_rate * (average + outer_beta * momentum_next)
    shared_next = lax.all_gather(master_next.astype(jnp.bfloat16), "replica", axis=1, tiled=True)
    stepped = weight_float - inner_rate * grad
    layer_next = (
        mix_weight * stepped + (1.0 - mix_weight) * shared_next.astype(jnp.float32)
    ).astype(jnp.bfloat16)
    return (layer_next[None], master_next, momentum_next)


def solution(mesh):
    in_specs = (
        P("replica", "fsdp", None),
        P(),
        P("replica", "fsdp", None),
        P("replica", "fsdp", None),
        P("fsdp", None),
        P("fsdp", "replica"),
        P("fsdp", "replica"),
    )
    out_specs = (P("replica", "fsdp", None), P("fsdp", "replica"), P("fsdp", "replica"))
    return jax.shard_map(
        on_device, mesh=mesh, in_specs=in_specs, out_specs=out_specs, check_vma=False
    )
```

profile of v0, /device:TPU:6, one launch (start us, length us, event | category | flops | bytes accessed | tf_op | source)
XLA Modules:
  0.0 382.0 jit_solution(5349292142354110479)
XLA Ops:
  8.0 0.0 reduce-scatter.2.cloned.1.call-start
  8.0 1.4 convert_subtract_fusion
  9.4 0.3 copy.30
  9.8 0.0 copy-start.4
  9.8 0.1 abs_reduce_fusion
  9.9 0.1 divide_convert_fusion
  10.0 0.9 multiply_convert_fusion.1
  10.9 0.0 reduce-scatter.2.cloned.1.call-update
  10.9 0.0 all-gather.3.cloned.1.call-start
  11.0 0.5 all-gather.3.cloned.1.call-update
  11.5 3.2 copy.28
  14.7 0.0 copy-done.4
  14.8 1.1 multiply_reduce_fusion
  15.9 0.0 copy-start.2
  15.9 0.0 copy-start.3
  15.9 2.2 multiply_convert_fusion
  18.1 0.0 copy-start.1
  18.1 15.7 %all-to-all-start = ((bf16[128,32,256]{0,2,1:T(8,128)(2,1)}), bf16[128,32,256]{0,2,1:T(8,128)(2,1)S(1)}, u32[]{:S(2)}, u32[]{:S(2)}) async-start(bf16[128,32,256]{0,2,1:T(8,128)(2,1)} %multiply_convert_fusion), calls=%async_computation | async-start | bytes 4194304 | tf_op jit(solution)/shard_map/all_to_all | solution.py:23
  33.8 113.7 %reduce-scatter.2.cloned.1.call-done = bf16[256,1,64]{0,2,1:T(8,128)(2,1)} async-done(((bf16[256,16,64]{0,2,1:T(8,128)(2,1)}), bf16[256,1,64]{0,2,1:T(8,128)(2,1)}) %reduce-scatter.2.cloned.1.call-update) | async-done | bytes 32784 | tf_op jit(solution)/shard_map/reduce_scatter | solution.py:43
  147.5 0.0 copy-done.2
  147.5 0.0 copy-done.3
  147.5 1.4 fusion.22
  148.9 39.1 %all_gather.7 = bf16[256,1024]{0,1:T(8,128)(2,1)} all-gather(bf16[256,64]{0,1:T(8,128)(2,1)S(1)} %get-tuple-element.12), channel_id=1, replica_groups=mesh['replica'=16,'fsdp'=32] {'replica'}, dimensions={1}, use_global_device_ids=true | all-gather | bytes 557056 | tf_op jit(solution)/shard_map/all_gather | solution.py:49
  188.0 1.2 copy.31
  189.3 15.4 %all-to-all-done = bf16[128,32,256]{0,2,1:T(8,128)(2,1)S(1)} async-done(((bf16[128,32,256]{0,2,1:T(8,128)(2,1)}), bf16[128,32,256]{0,2,1:T(8,128)(2,1)S(1)}, u32[]{:S(2)}, u32[]{:S(2)}) %all-to-all-start) | async-done | bytes 2097184 | tf_op jit(solution)/shard_map/all_to_all | solution.py:23
  204.7 0.0 copy-start
  204.7 1.4 copy-done
  206.1 3.3 copy.29
  209.3 158.6 %all-gather.3.cloned.1.call-done = bf16[1,4096,1024]{2,1,0:T(8,128)(2,1)} async-done(((bf16[1,128,1024]{2,1,0:T(8,128)(2,1)}), bf16[1,4096,1024]{2,1,0:T(8,128)(2,1)}) %all-gather.3.cloned.1.call-update) | async-done | bytes 8388624 | tf_op jit(solution)/shard_map/all_gather | solution.py:29
  367.9 0.0 copy-done.1
  367.9 6.6 %fusion.16 = bf16[1,256,1024]{2,1,0:T(8,128)(2,1)} fusion(bf16[4096,256]{1,0:T(8,128)(2,1)S(1)} %bitcast.39, bf16[1,4096,1024]{2,1,0:T(8,128)(2,1)} %all-gather.3.cloned.1.call-done, bf16[256,1024]{1,0:T(8,128)(2,1)S(1)} %copy.31, bf16[1,256,1024]{2,1,0:T(8,128)(2,1)S(1)} %copy-done.1), kind=kOutput, calls=%fused_computation.10 | convolution fusion | flops 2149318656 | bytes 12058624 | tf_op jit(solution)/shard_map/dot_general | solution.py:27
  (3 shorter events, 0.0 us)
Async XLA Ops:
  8.0 139.5 %reduce-scatter.2.cloned.1.call-start = ((), (), s32[]{:S(2)}) async-start(), calls=%async_computation.2 | async-start | bytes 557056 | tf_op jit(solution)/shard_map/reduce_scatter | solution.py:43
  9.8 5.0 %copy-start.4 = (bf16[8192]{0:T(1024)(128)(2,1)S(1)}, bf16[8192]{0:T(1024)(128)(2,1)}, u32[]{:S(2)}) copy-start(bf16[8192]{0:T(1024)(128)(2,1)} %param.8) | copy-start | bytes 49156
  10.9 357.0 %all-gather.3.cloned.1.call-start = ((), (), s32[]{:S(2)}) async-start(), calls=%async_computation.3 | async-start | bytes 8650752 | tf_op jit(solution)/shard_map/all_gather | solution.py:29
  15.9 131.6 %copy-start.2 = (f32[256,64]{0,1:T(8,128)S(1)}, f32[256,64]{0,1:T(8,128)}, u32[]{:S(2)}) copy-start(f32[256,64]{0,1:T(8,128)} %param.12) | copy-start | bytes 196612
  15.9 131.6 %copy-start.3 = (f32[256,64]{0,1:T(8,128)S(1)}, f32[256,64]{0,1:T(8,128)}, u32[]{:S(2)}) copy-start(f32[256,64]{0,1:T(8,128)} %param.13) | copy-start | bytes 196612
  18.1 349.8 %copy-start.1 = (bf16[1,256,1024]{2,1,0:T(8,128)(2,1)S(1)}, bf16[1,256,1024]{2,1,0:T(8,128)(2,1)}, u32[]{:S(2)}) copy-start(bf16[1,256,1024]{2,1,0:T(8,128)(2,1)} %param.10) | copy-start | bytes 1572868
  18.1 186.6 %all-to-all-start = ((bf16[128,32,256]{0,2,1:T(8,128)(2,1)}), bf16[128,32,256]{0,2,1:T(8,128)(2,1)S(1)}, u32[]{:S(2)}, u32[]{:S(2)}) async-start(bf16[128,32,256]{0,2,1:T(8,128)(2,1)} %multiply_convert_fusion), calls=%async_computation | async-start | bytes 4194304 | tf_op jit(solution)/shard_map/all_to_all | solution.py:23
  204.7 1.4 copy-start
Sparse Core Ops, SparseCore 0:
  14.0 133.4 reduce-scatter.1
Sparse Core Ops, SparseCore 1:
  13.5 354.4 all-gather.2
where the time goes:
time: 382 us
  waiting for transfers between devices  288 us (75%)
  blocking collectives  39.1 us (10%)
  starting transfers between devices  15.8 us (4%)
  between operations  15.6 us (4%)
  local copies, waits for them, and re-layouts  9.46 us (2%)
  other arithmetic  7.22 us (2%)
  matrix products  6.62 us (2%)
    all_gather x1, waiting for transfers between devices, on_device(): lax.all_gather(cotangent[0], 'fsdp', axis=0, tiled=True)  159 us
    reduce_scatter x1, waiting for transfers between devices, on_device(): lax.psum_scatter(decoded.astype(jnp.bfloat16), 'replica', scatter_dimensi...  114 us
    all_gather x1, blocking collectives, on_device(): lax.all_gather(master_next.astype(jnp.bfloat16), 'replica', axis=1, tiled...  39.1 us
    all_to_all x1, starting transfers between devices, on_device(): lax.all_to_all(normed, 'fsdp', split_axis=1, concat_axis=0, tiled=True)  15.7 us
    all_to_all x1, waiting for transfers between devices, on_device(): lax.all_to_all(normed, 'fsdp', split_axis=1, concat_axis=0, tiled=True)  15.4 us
  transfers between devices with their start and end apart: 3, of which 3 were waited for; matrix products, arithmetic and copies ran while one was open for 3% of the time, Pallas kernels for 0%

commit v1 on v0

v1 whole, which is shorter than its diff:
```python
import functools
import math

import jax
import jax.numpy as jnp
from jax import lax
from jax.experimental import pallas as pl
from jax.experimental.pallas import tpu as pltpu
from jax.sharding import PartitionSpec as P

BLOCK = 64
norm_eps = 1e-05
inner_gain = 0.4
outer_rate = 0.7
outer_beta = 0.9
mix_weight = 0.5
code_range = 448.0

NX, NY, NZ = 4, 4, 8
REPLICAS = 16
MESH = pl.DeviceIdType.MESH
F32, BF16 = jnp.float32, jnp.bfloat16
COLS = 256
SUBS = 4
UNITS = (NZ - 1) * SUBS
DEPTH = 3


def kernel(
    tok_hbm, gain_ref, cot_hbm, w_hbm, shared_hbm, master_hbm, mom_hbm,
    layer_out, master_out, mom_out,
    tok, cot, w, shared, master, mom,
    tokg, cotg, buf_f, buf_b, dec, x_in, half, core_out, core_in, z_out, z_in,
    full, pair_out, pair_in, sh, sh_in,
    load_sem, st, rt, sc, rc, sf, rf, sb, rb, sx, rx, sg, rg, ss, rs,
):
    rep, fs = lax.axis_index("replica"), lax.axis_index("fsdp")
    x, zh, c = rep // 4, lax.rem(rep // 2, 2), lax.rem(rep, 2)
    y, z = fs // NZ, lax.rem(fs, NZ)

    def device(x=x, zh=zh, c=c, y=y, z=z):
        return (x * 4 + zh * 2 + c, y * NZ + z)

    def y_peer(k):
        return lax.rem(y + k, NY)

    def x_peer(k):
        return lax.rem(x + k, NX)

    loads = [
        pltpu.make_async_copy(src, dst, load_sem.at[i])
        for i, (src, dst) in enumerate(
            [(tok_hbm, tok), (cot_hbm, cot), (w_hbm, w), (shared_hbm, shared),
             (master_hbm, master), (mom_hbm, mom)]
        )
    ]
    for load in loads:
        load.start()

    barrier = pltpu.get_barrier_semaphore()

    def greet(where):
        pl.semaphore_signal(barrier, inc=1, device_id=where, device_id_type=MESH)

    for k in (1, 2, 3):
        greet(device(y=y_peer(k)))
        greet(device(x=x_peer(k)))
    greet(device(c=1 - c))
    greet(device(zh=1 - zh))

    @pl.when(z > 0)
    def _():
        greet(device(z=z - 1))

    @pl.when(z < NZ - 1)
    def _():
        greet(device(z=z + 1))

    def remote(src, dst, send, recv, where):
        return pltpu.make_async_remote_copy(
            src_ref=src, dst_ref=dst, send_sem=send, recv_sem=recv, device_id=where, device_id_type=MESH
        )

    def order(i):
        near = i // 2
        flip = lax.rem(i, 2) == jnp.where(z < NZ // 2, 0, 1)
        return jnp.where(flip, NZ - 1 - near, near)

    def my_rows():
        return pl.ds(pl.multiple_of(y * 128, 128), 128)

    def columns_of(peer, d):
        return pl.ds(pl.multiple_of((peer * NZ + d) * COLS, COLS), COLS)

    def token_copy(d, k):
        peer = y_peer(k)
        return remote(
            tok.at[:, columns_of(peer, d)], tokg.at[d, my_rows()], st.at[d, k - 1], rt.at[d, k - 1], device(y=peer)
        )

    def cot_copy(q, k):
        return remote(
            cotg.at[q, my_rows()], cotg.at[q, my_rows()], sc.at[q, k - 1], rc.at[q, k - 1], device(y=y_peer(k))
        )

    def send_tokens(d):
        for k in (1, 2, 3):
            token_copy(d, k).start()

    def wait_tokens(d):
        for k in (1, 2, 3):
            token_copy(d, k).wait_recv()

    loads[0].wait()
    pl.semaphore_wait(barrier, 8 + jnp.where(z > 0, 1, 0) + jnp.where(z < NZ - 1, 1, 0))
    send_tokens(order(0))

    def square(j, acc):
        t = tok[:, pl.ds(pl.multiple_of(j * 128, 128), 128)].astype(F32)
        return acc + t * t

    total = lax.fori_loop(0, 64, square, jnp.zeros((128, 128), F32), unroll=8)
    inverse = lax.rsqrt(jnp.sum(total, axis=1, keepdims=True) / 8192.0 + norm_eps)
    loads[1].wait()
    for q in range(SUBS):
        cotg[q, my_rows(), :] = (cot[:, q * COLS : (q + 1) * COLS].astype(F32) * inverse).astype(BF16)
        for k in (1, 2, 3):
            cot_copy(q, k).start()
    send_tokens(order(1))

    def keep(d, _):
        tokg[d, my_rows(), :] = tok[:, columns_of(y, d)]
        return 0

    lax.fori_loop(0, NZ, keep, 0)

    loads[2].wait()
    loads[3].wait()
    low = lax.broadcasted_iota(jnp.int32, (256, 128), 1) < BLOCK

    def decode(t, _):
        at = pl.ds(pl.multiple_of(t * 128, 128), 128)
        delta = shared[:, at].astype(F32) - w[:, at].astype(F32)
        size = jnp.abs(delta)
        first = jnp.max(jnp.where(low, size, 0.0), axis=1, keepdims=True)
        second = jnp.max(jnp.where(low, 0.0, size), axis=1, keepdims=True)
        largest = jnp.where(low, first, second)
        scale = ((largest + 1e-06) / code_range).astype(BF16).astype(F32)
        coded = (delta / scale).astype(BF16).astype(F32)
        dec[t // 2, :, pl.ds(pl.multiple_of(lax.rem(t, 2) * 128, 128), 128)] = (coded * scale).astype(BF16)
        return 0

    lax.fori_loop(0, 8, decode, 0)

    def scatter_copy(k):
        peer = x_peer(k)
        return remote(dec.at[peer], x_in.at[k - 1], sx.at[k - 1], rx.at[k - 1], device(x=peer))

    for k in (1, 2, 3):
        scatter_copy(k).start()

    mine = pl.ds(pl.multiple_of(c * 128, 128), 128)
    other = pl.ds(pl.multiple_of((1 - c) * 128, 128), 128)
    my_lanes = pl.ds(pl.multiple_of(zh * 128, 128), 128)
    far_lanes = pl.ds(pl.multiple_of((1 - zh) * 128, 128), 128)
    core = device(c=1 - c)
    far = device(zh=1 - zh)
    core_sum = remote(core_out, core_in, ss.at[0], rs.at[0], core)
    z_sum = remote(z_out, z_in, ss.at[1], rs.at[1], far)
    core_full = remote(full.at[mine], full.at[mine], ss.at[2], rs.at[2], core)
    core_pair = remote(pair_out, pair_in, ss.at[3], rs.at[3], core)
    z_gather = remote(sh.at[x, mine, my_lanes], sh.at[x, mine, my_lanes], ss.at[4], rs.at[4], far)
    core_gather = remote(sh.at[:, mine], sh_in, ss.at[5], rs.at[5], core)

    def gather_copy(k):
        return remote(sh.at[x, mine], sh.at[x, mine], sg.at[k - 1], rg.at[k - 1], device(x=x_peer(k)))

    def stage_x():
        for k in (1, 2, 3):
            scatter_copy(k).wait_recv()

        def summed(rows):
            acc = dec[x, rows, :].astype(F32)
            for k in range(3):
                acc = acc + x_in[k, rows, :].astype(F32)
            return acc

        core_out[...] = summed(other).astype(BF16)
        core_sum.start()
        half[...] = summed(mine)

    def stage_core():
        core_sum.wait_recv()
        half[...] = half[...] + core_in[...].astype(F32)
        z_out[...] = half[:, far_lanes].astype(BF16)
        z_sum.start()

    def stage_far():
        z_sum.wait_recv()
        full[mine, :] = half[:, my_lanes] + z_in[...].astype(F32)
        core_full.start()

    def stage_update():
        core_full.wait_recv()
        loads[4].wait()
        loads[5].wait()
        average = full[...] / float(REPLICAS)
        average = jnp.where(c == 0, average[:, :BLOCK], average[:, BLOCK:])
        momentum_next = outer_beta * mom[...] + average
        master_next = master[...] - outer_rate * (average + outer_beta * momentum_next)
        mom_out[...] = momentum_next
        master_out[...] = master_next
        twice = jnp.concatenate([master_next, master_next], axis=1)
        lanes = lax.broadcasted_iota(jnp.int32, (256, 128), 1) // BLOCK
        pair_out[...] = jnp.where(lanes == c, twice, 0.0).astype(BF16)
        core_pair.start()

    def stage_pair():
        core_pair.wait_recv()
        sh[x, :, my_lanes] = pair_out[...] + pair_in[...]
        z_gather.start()

    def stage_gather():
        z_gather.wait_recv()
        for k in (1, 2, 3):
            gather_copy(k).start()

    def stage_last():
        for k in (1, 2, 3):
            gather_copy(k).wait_recv()
        core_gather.start()

    stages = {1: stage_x, 2: stage_core, 7: stage_far, 8: stage_update, 9: stage_pair, 15: stage_gather, 17: stage_last}

    def product(d, q):
        return lax.dot_general(tokg[d], cotg[q], (((0,), (0,)), ((), ())), preferred_element_type=F32)

    count_f = SUBS * (NZ - 1 - z)
    count_b = SUBS * z
    lag_f = jnp.where(z < NZ // 2, 0, 4 * z - 10)
    lag_b = jnp.where(z < NZ // 2, 18 - 4 * z, 0)

    def forward(u):
        s, q = u // SUBS, lax.rem(u, SUBS)
        return remote(buf_f.at[s, q], buf_f.at[s, q], sf.at[u], rf.at[u], device(z=z + 1))

    def backward(u):
        s, q = u // SUBS, lax.rem(u, SUBS)
        return remote(buf_b.at[s, q], buf_b.at[s, q], sb.at[u], rb.at[u], device(z=z - 1))

    def unit(u, d, first, buf, copy):
        s, q = u // SUBS, lax.rem(u, SUBS)

        @pl.when(q == 0)
        def _():
            wait_tokens(d)

        part = product(d, q)

        @pl.when(first)
        def _():
            buf[s, q] = part.astype(BF16)

        @pl.when(jnp.logical_not(first))
        def _():
            copy(u).wait_recv()
            buf[s, q] = (part + buf[s, q].astype(F32)).astype(BF16)

        @pl.when(u >= DEPTH)
        def _():
            copy(u - DEPTH).wait_send()

        copy(u).start()

    def step(u, _):
        @pl.when(u < SUBS)
        def _():
            for k in (1, 2, 3):
                cot_copy(u, k).wait_recv()

        uf = u - lag_f
        ub = u - lag_b

        @pl.when((uf >= 0) & (uf < count_f))
        def _():
            unit(uf, NZ - 1 - uf // SUBS, z == 0, buf_f, forward)

        @pl.when((ub >= 0) & (ub < count_b))
        def _():
            unit(ub, ub // SUBS, z == NZ - 1, buf_b, backward)

        @pl.when(u < NZ - 2)
        def _():
            send_tokens(order(u + 2))

        for at, stage in stages.items():
            pl.when(u == at)(stage)
        return 0

    lax.fori_loop(0, UNITS, step, 0)

    wait_tokens(z)
    core_gather.wait_recv()
    for q in range(SUBS):
        sh[q, other, :] = sh_in[q]
    row = lax.broadcasted_iota(jnp.int32, (64, 128), 0)
    gain = gain_ref[...].astype(F32)
    tall = [
        jnp.transpose(
            jnp.broadcast_to(
                jnp.sum(jnp.where(row == 2 * fs + h, gain, 0.0), axis=0, keepdims=True), (128, 128)
            )
        )
        for h in range(2)
    ]
    tall = jnp.concatenate(tall, axis=0)
    rate = tall[:, :1] * (mix_weight * inner_gain / math.sqrt(32 * 128))
    for q in range(SUBS):
        full_sum = product(z, q)
        half_w = mix_weight * w[:, q * COLS : (q + 1) * COLS].astype(F32) + (1.0 - mix_weight) * sh[q].astype(F32)

        @pl.when(z > 0)
        def _():
            forward((NZ - 1 - z) * SUBS + q).wait_recv()

        @pl.when(z < NZ - 1)
        def _():
            backward(z * SUBS + q).wait_recv()

        near_f = jnp.minimum(NZ - 1 - z, NZ - 2)
        near_b = jnp.minimum(z, NZ - 2)
        left = jnp.where(z > 0, buf_f[near_f, q].astype(F32), 0.0)
        right = jnp.where(z < NZ - 1, buf_b[near_b, q].astype(F32), 0.0)
        layer_out[:, q * COLS : (q + 1) * COLS] = (half_w - rate * (full_sum + left + right)).astype(BF16)

    for k in (1, 2, 3):
        for d in range(NZ):
            token_copy(d, k).wait_send()
        for q in range(SUBS):
            cot_copy(q, k).wait_send()
        scatter_copy(k).wait_send()
        gather_copy(k).wait_send()
    for copy in (core_sum, z_sum, core_full, core_pair, z_gather, core_gather):
        copy.wait_send()

    @pl.when(z < NZ - 1)
    def _():
        for back in range(DEPTH):
            forward(count_f - 1 - back).wait_send()

    @pl.when(z > 0)
    def _():
        for back in range(DEPTH):
            backward(count_b - 1 - back).wait_send()


def on_device(tokens, norm_gain, cotangent, layer_weight, shared_copy, master, momentum):
    vmem, hbm = pltpu.VMEM, pl.ANY
    dma = pltpu.SemaphoreType.DMA
    scratch = [
        vmem((128, 8192), BF16), vmem((128, 1024), BF16), vmem((256, 1024), BF16), vmem((256, 1024), BF16),
        vmem((256, 64), F32), vmem((256, 64), F32),
        vmem((NZ, 512, COLS), BF16), vmem((SUBS, 512, COLS), BF16),
        vmem((NZ - 1, SUBS, 256, COLS), BF16), vmem((NZ - 1, SUBS, 256, COLS), BF16),
        vmem((4, 256, 256), BF16), vmem((3, 256, 256), BF16), vmem((128, 256), F32),
        vmem((128, 256), BF16), vmem((128, 256), BF16), vmem((128, 128), BF16), vmem((128, 128), BF16),
        vmem((256, 128), F32), vmem((256, 128), BF16), vmem((256, 128), BF16),
        vmem((4, 256, 256), BF16), vmem((4, 128, 256), BF16),
        dma((6,)),
        dma((NZ, 3)), dma((NZ, 3)), dma((SUBS, 3)), dma((SUBS, 3)),
        dma((UNITS,)), dma((UNITS,)), dma((UNITS,)), dma((UNITS,)),
        dma((3,)), dma((3,)), dma((3,)), dma((3,)), dma((6,)), dma((6,)),
    ]
    layer_next, master_next, momentum_next = pl.pallas_call(
        kernel,
        out_shape=[
            jax.ShapeDtypeStruct((256, 1024), BF16),
            jax.ShapeDtypeStruct((256, 64), F32),
            jax.ShapeDtypeStruct((256, 64), F32),
        ],
        in_specs=[pl.BlockSpec(memory_space=hbm), pl.BlockSpec(memory_space=vmem)]
        + [pl.BlockSpec(memory_space=hbm)] * 5,
        out_specs=[pl.BlockSpec(memory_space=vmem)] * 3,
        scratch_shapes=scratch,
        name="diloco_step",
        cost_estimate=pl.CostEstimate(flops=2 * 4096 * 256 * 1024, bytes_accessed=5 << 20, transcendentals=0),
        compiler_params=pltpu.CompilerParams(
            collective_id=0, has_side_effects=True, vmem_limit_bytes=48 << 20
        ),
    )(
        tokens[0], norm_gain.reshape(64, 128), cotangent[0], layer_weight[0], shared_copy, master, momentum
    )
    return (layer_next[None], master_next, momentum_next)


def solution(mesh):
    in_specs = (
        P("replica", "fsdp", None),
        P(),
        P("replica", "fsdp", None),
        P("replica", "fsdp", None),
        P("fsdp", None),
        P("fsdp", "replica"),
        P("fsdp", "replica"),
    )
    out_specs = (P("replica", "fsdp", None), P("fsdp", "replica"), P("fsdp", "replica"))
    return jax.shard_map(
        on_device, mesh=mesh, in_specs=in_specs, out_specs=out_specs, check_vma=False
    )
```

time: 382 us -> 123 us (0.32)
  waiting for transfers between devices: 288 us -> 0 us
  Pallas kernels: 0 us -> 112 us
  blocking collectives: 39.1 us -> 0 us
  starting transfers between devices: 15.8 us -> 0 us
  between operations: 15.6 us -> 0.66 us
  other arithmetic: 7.22 us -> 0 us
  matrix products: 6.62 us -> 0 us
    all_gather x1 -> x0, waiting for transfers between devices: 159 us -> none  [on_device(): lax.all_gather(cotangent[0], 'fsdp', axis=0, tiled=True)]
    reduce_scatter x1 -> x0, waiting for transfers between devices: 114 us -> none  [on_device(): lax.psum_scatter(decoded.astype(jnp.bfloat16), 'replica', scatter_dimensi...]
    pallas_call x0 -> x1, Pallas kernels: none -> 112 us  [on_device(): pl.pallas_call(kernel, out_shape=[jax.ShapeDtypeStruct((256, 1024), BF16)...]
    all_gather x1 -> x0, blocking collectives: 39.1 us -> none  [on_device(): lax.all_gather(master_next.astype(jnp.bfloat16), 'replica', axis=1, tiled...]
    all_to_all x1 -> x0, starting transfers between devices: 15.7 us -> none  [on_device(): lax.all_to_all(normed, 'fsdp', split_axis=1, concat_axis=0, tiled=True)]
    all_to_all x1 -> x0, waiting for transfers between devices: 15.4 us -> none  [on_device(): lax.all_to_all(normed, 'fsdp', split_axis=1, concat_axis=0, tiled=True)]
    dot_general x1 -> x0, matrix products: 6.62 us -> none  [on_device(): lax.dot_general(columns, lax.all_gather(cotangent[0], 'fsdp', axis=0, til...]
    unnamed x11 -> x15, local copies, waits for them, and re-layouts: 4.61 us -> 9.42 us
  transfers between devices with their start and end apart: 3 -> 0, of which waited for: 3 -> 0; matrix products, arithmetic and copies ran while one was open for 3% -> 0% of each run, Pallas kernels for 0% -> 0%
where the time goes in v1:
time: 123 us; the launch traced here: 122 us
  Pallas kernels  112 us (91%)
  local copies, waits for them, and re-layouts  9.42 us (8%)
    pallas_call x1, Pallas kernels, on_device(): pl.pallas_call(kernel, out_shape=[jax.ShapeDtypeStruct((256, 1024), BF16)...  112 us
    unnamed x15, local copies, waits for them, and re-layouts  9.42 us

profile of v1, /device:TPU:6, one launch (start us, length us, event | category | flops | bytes accessed | tf_op | source)
XLA Modules:
  0.0 121.9 jit_solution(14548352275578017039)
XLA Ops:
  0.6 0.9 copy.10.master_hbm
  1.6 0.9 copy.11.mom_hbm
  2.5 0.0 copy-start
  2.5 1.6 %copy-done = bf16[1,128,8192]{2,1,0:T(8,128)(2,1)S(1)} copy-done((bf16[1,128,8192]{2,1,0:T(8,128)(2,1)S(1)}, bf16[1,128,8192]{2,1,0:T(8,128)(2,1)}, u32[]{:S(2)}) %copy-start) | copy-done | bytes 2097176
  4.1 0.0 copy-start.1
  4.1 1.0 copy-done.1
  5.1 0.0 copy-start.2
  5.1 1.0 copy-done.2
  6.2 0.0 copy-start.3
  6.2 0.9 copy-done.3
  7.1 0.0 copy-start.4
  7.1 0.7 copy-done.4
  7.9 111.9 %diloco_step.1 = (bf16[256,1024]{1,0:T(8,128)(2,1)S(1)}, f32[256,64]{1,0:T(8,128)S(1)}, f32[256,64]{1,0:T(8,128)S(1)}) custom-call(bf16[128,8192]{1,0:T(8,128)(2,1)S(1)} %bitcast.6, bf16[64,128]{1,0:T(8,128)(2,1)S(1)} %bitcast.9, bf16[128,1024]{1,0:T(8,128)(2,1)S(1)} %bitcast.8, bf16[256,1024]{1,0:T(8,128)(2,1)S(1)} %bitcast.7, ...), custom_call_target="tpu_custom_call" | custom-call | flops 2147483648 | bytes 5242880 | tf_op jit(solution)/shard_map/diloco_step/pallas_call | solution.py:374
  119.7 0.7 copy.12
  120.4 0.7 copy.13
  121.2 0.8 copy.15
Async XLA Ops:
  2.5 1.6 %copy-start = (bf16[1,128,8192]{2,1,0:T(8,128)(2,1)S(1)}, bf16[1,128,8192]{2,1,0:T(8,128)(2,1)}, u32[]{:S(2)}) copy-start(bf16[1,128,8192]{2,1,0:T(8,128)(2,1)} %param.7) | copy-start | bytes 6291460
  4.1 1.0 copy-start.1
  5.1 1.0 copy-start.2
  6.2 0.9 copy-start.3
  7.1 0.7 copy-start.4

commit v2 on v1

--- a/solution.py
+++ b/solution.py
@@ -29,17 +29,26 @@
 def kernel(
     tok_hbm, gain_ref, cot_hbm, w_hbm, shared_hbm, master_hbm, mom_hbm,
     layer_out, master_out, mom_out,
-    tok, cot, w, shared, master, mom,
-    tokg, cotg, buf_f, buf_b, dec, x_in, half, core_out, core_in, z_out, z_in,
+    tok, cot, w, shared, master, mom, layer, master_new, mom_new,
+    tokg, cotg, buf, acc, tok_edge, cot_edge, dec, x_in, half, core_out, core_in, z_out, z_in,
     full, pair_out, pair_in, sh, sh_in,
-    load_sem, st, rt, sc, rc, sf, rf, sb, rb, sx, rx, sg, rg, ss, rs,
+    load_sem, st, rt, sc, rc, su, ru, ste, rte, sce, rce, sye, rye, sx, rx, sg, rg, ss, rs, out_sem, wave_up, wave_down,
 ):
     rep, fs = lax.axis_index("replica"), lax.axis_index("fsdp")
     x, zh, c = rep // 4, lax.rem(rep // 2, 2), lax.rem(rep, 2)
     y, z = fs // NZ, lax.rem(fs, NZ)
+    line = zh * NZ + z
+    last = 2 * NZ - 1
+    low_half = z < NZ // 2
+    depth = jnp.where(low_half, z, NZ - 1 - z)
+    inward = jnp.where(low_half, z + 1, z - 1)
+    edge, second = depth == 0, depth == 1
 
     def device(x=x, zh=zh, c=c, y=y, z=z):
         return (x * 4 + zh * 2 + c, y * NZ + z)
+
+    def on_line(at):
+        return device(zh=at // NZ, z=lax.rem(at, NZ))
 
     def y_peer(k):
         return lax.rem(y + k, NY)
@@ -54,9 +63,8 @@
              (master_hbm, master), (mom_hbm, mom)]
         )
     ]
-    for load in loads:
-        load.start()
-
+    loads[0].start()
+    loads[1].start()
     barrier = pltpu.get_barrier_semaphore()
 
     def greet(where):
@@ -66,25 +74,25 @@
         greet(device(y=y_peer(k)))
         greet(device(x=x_peer(k)))
     greet(device(c=1 - c))
-    greet(device(zh=1 - zh))
-
-    @pl.when(z > 0)
-    def _():
-        greet(device(z=z - 1))
-
-    @pl.when(z < NZ - 1)
-    def _():
-        greet(device(z=z + 1))
+
+    @pl.when(line > 0)
+    def _():
+        greet(on_line(line - 1))
+
+    @pl.when(line < last)
+    def _():
+        greet(on_line(line + 1))
 
     def remote(src, dst, send, recv, where):
         return pltpu.make_async_remote_copy(
             src_ref=src, dst_ref=dst, send_sem=send, recv_sem=recv, device_id=where, device_id_type=MESH
         )
 
+    def dest(s):
+        return jnp.where(low_half, NZ - 1 - s, s)
+
     def order(i):
-        near = i // 2
-        flip = lax.rem(i, 2) == jnp.where(z < NZ // 2, 0, 1)
-        return jnp.where(flip, NZ - 1 - near, near)
+        return jnp.where(lax.rem(i, 2) == 0, 1 + i // 2, NZ - 1 - (i - 3) // 2)
 
     def my_rows():
         return pl.ds(pl.multiple_of(y * 128, 128), 128)
@@ -112,8 +120,10 @@
             token_copy(d, k).wait_recv()
 
     loads[0].wait()
-    pl.semaphore_wait(barrier, 8 + jnp.where(z > 0, 1, 0) + jnp.where(z < NZ - 1, 1, 0))
-    send_tokens(order(0))
+    pl.semaphore_wait(barrier, 7 + jnp.where(line > 0, 1, 0) + jnp.where(line < last, 1, 0))
+    send_tokens(dest(0))
+    for load in loads[2:]:
+        load.start()
 
     def square(j, acc):
         t = tok[:, pl.ds(pl.multiple_of(j * 128, 128), 128)].astype(F32)
@@ -126,7 +136,44 @@
         cotg[q, my_rows(), :] = (cot[:, q * COLS : (q + 1) * COLS].astype(F32) * inverse).astype(BF16)
         for k in (1, 2, 3):
             cot_copy(q, k).start()
-    send_tokens(order(1))
+    send_tokens(dest(1))
+
+    def edge_cot(q):
+        return remote(
+            cotg.at[q, my_rows()], cot_edge.at[q, my_rows()], sce.at[q], rce.at[q], device(z=inward)
+        )
+
+    def edge_relay(q, k):
+        return remote(
+            cot_edge.at[q, my_rows()], cot_edge.at[q, my_rows()], sye.at[q, k - 1], rye.at[q, k - 1],
+            device(y=y_peer(k)),
+        )
+
+    def edge_tokens(s):
+        return remote(tokg.at[dest(s)], tok_edge.at[s - 1], ste.at[s - 1], rte.at[s - 1], device(z=inward))
+
+    @pl.when(edge)
+    def _():
+        for q in range(SUBS):
+            edge_cot(q).start()
+
+    def pass_up():
+        @pl.when(line > 0)
+        def _():
+            pl.semaphore_wait(wave_up, 1)
+
+        @pl.when(line < last)
+        def _():
+            pl.semaphore_signal(wave_up, inc=1, device_id=on_line(line + 1), device_id_type=MESH)
+
+    def pass_down():
+        @pl.when(line < last)
+        def _():
+            pl.semaphore_wait(wave_down, 1)
+
+        @pl.when(line > 0)
+        def _():
+            pl.semaphore_signal(wave_down, inc=1, device_id=on_line(line - 1), device_id_type=MESH)
 
     def keep(d, _):
         tokg[d, my_rows(), :] = tok[:, columns_of(y, d)]
@@ -158,6 +205,16 @@
 
     for k in (1, 2, 3):
         scatter_copy(k).start()
+
+    near_half = zh == 0
+    pl.when(near_half)(pass_up)
+
+    @pl.when(second)
+    def _():
+        for q in range(SUBS):
+            edge_cot(q).wait_recv()
+            for k in (1, 2, 3):
+                edge_relay(q, k).start()
 
     mine = pl.ds(pl.multiple_of(c * 128, 128), 128)
     other = pl.ds(pl.multiple_of((1 - c) * 128, 128), 128)
@@ -175,6 +232,11 @@
     def gather_copy(k):
         return remote(sh.at[x, mine], sh.at[x, mine], sg.at[k - 1], rg.at[k - 1], device(x=x_peer(k)))
 
+    stores = [
+        pltpu.make_async_copy(src, dst, out_sem.at[i])
+        for i, (src, dst) in enumerate([(master_new, master_out), (mom_new, mom_out)])
+    ]
+
     def stage_x():
         for k in (1, 2, 3):
             scatter_copy(k).wait_recv()
@@ -204,15 +266,17 @@
         core_full.wait_recv()
         loads[4].wait()
         loads[5].wait()
-        average = full[...] / float(REPLICAS)
-        average = jnp.where(c == 0, average[:, :BLOCK], average[:, BLOCK:])
+        average = jnp.transpose(full[...]) / float(REPLICAS)
+        average = jnp.where(c == 0, average[:BLOCK], average[BLOCK:])
         momentum_next = outer_beta * mom[...] + average
         master_next = master[...] - outer_rate * (average + outer_beta * momentum_next)
-        mom_out[...] = momentum_next
-        master_out[...] = master_next
-        twice = jnp.concatenate([master_next, master_next], axis=1)
-        lanes = lax.broadcasted_iota(jnp.int32, (256, 128), 1) // BLOCK
-        pair_out[...] = jnp.where(lanes == c, twice, 0.0).astype(BF16)
+        mom_new[...] = momentum_next
+        master_new[...] = master_next
+        stores[0].start()
+        stores[1].start()
+        twice = jnp.concatenate([master_next, master_next], axis=0)
+        share = lax.broadcasted_iota(jnp.int32, (128, 256), 0) // BLOCK
+        pair_out[...] = jnp.transpose(jnp.where(share == c, twice, 0.0)).astype(BF16)
         core_pair.start()
 
     def stage_pair():
@@ -230,47 +294,96 @@
             gather_copy(k).wait_recv()
         core_gather.start()
 
-    stages = {1: stage_x, 2: stage_core, 7: stage_far, 8: stage_update, 9: stage_pair, 15: stage_gather, 17: stage_last}
-
-    def product(d, q):
-        return lax.dot_general(tokg[d], cotg[q], (((0,), (0,)), ((), ())), preferred_element_type=F32)
-
-    count_f = SUBS * (NZ - 1 - z)
-    count_b = SUBS * z
-    lag_f = jnp.where(z < NZ // 2, 0, 4 * z - 10)
-    lag_b = jnp.where(z < NZ // 2, 18 - 4 * z, 0)
-
-    def forward(u):
+    def pick(*choices):
+        at = choices[-1]
+        for i in range(len(choices) - 1):
+            at = jnp.where(depth == i, choices[i], at)
+        return at
+
+    up_at = jnp.where(z < 5, 0, jnp.where(z == 5, 2, jnp.where(z == 6, 4, 9)))
+    down_far = jnp.where(z > 2, 0, jnp.where(z == 2, 2, jnp.where(z == 1, 4, 9)))
+    down_near = jnp.where(low_half, pick(14, 9, 7, 5), pick(10, 6, 5, 4))
+    core_at = jnp.where(near_half, down_near, jnp.maximum(up_at, 2))
+    far_at = pick(15, 11, 10, 9)
+    gather_at = jnp.where(near_half, pick(21, 21, 20, 19), pick(19, 16, 16, 16))
+    stages = [
+        (1, stage_x),
+        (up_at, lambda: pl.when(jnp.logical_not(near_half))(pass_up)),
+        (jnp.where(near_half, down_near, down_far), pass_down),
+        (core_at, stage_core),
+        (far_at, stage_far),
+        (far_at + 1, stage_update),
+        (far_at + 2, stage_pair),
+        (gather_at, stage_gather),
+        (gather_at + 2, stage_last),
+    ]
+
+    def multiply(rows, q):
+        return lax.dot_general(rows, q, (((0,), (0,)), ((), ())), preferred_element_type=F32)
+
+    def stream(way, u):
         s, q = u // SUBS, lax.rem(u, SUBS)
-        return remote(buf_f.at[s, q], buf_f.at[s, q], sf.at[u], rf.at[u], device(z=z + 1))
-
-    def backward(u):
-        s, q = u // SUBS, lax.rem(u, SUBS)
-        return remote(buf_b.at[s, q], buf_b.at[s, q], sb.at[u], rb.at[u], device(z=z - 1))
-
-    def unit(u, d, first, buf, copy):
-        s, q = u // SUBS, lax.rem(u, SUBS)
-
-        @pl.when(q == 0)
-        def _():
-            wait_tokens(d)
-
-        part = product(d, q)
-
-        @pl.when(first)
-        def _():
-            buf[s, q] = part.astype(BF16)
-
-        @pl.when(jnp.logical_not(first))
-        def _():
-            copy(u).wait_recv()
-            buf[s, q] = (part + buf[s, q].astype(F32)).astype(BF16)
-
-        @pl.when(u >= DEPTH)
-        def _():
-            copy(u - DEPTH).wait_send()
-
-        copy(u).start()
+        to = jnp.where(way == 0, z + 1, z - 1)
+        return remote(buf.at[way, s, q], buf.at[way, s, q], su.at[way, u], ru.at[way, u], device(z=to))
+
+    count_in = jnp.where(edge, SUBS, SUBS * (NZ - 1 - depth))
+    count_out = SUBS * depth
+    inner = jnp.where(low_half, 0, 1)
+
+    def unit(k, u):
+        way = jnp.where(k == 0, inner, 1 - inner)
+        v = jnp.where(k == 0, u, u - (18 - 4 * depth))
+
+        @pl.when((v >= 0) & (v < jnp.where(k == 0, count_in, count_out)))
+        def _():
+            s, q = v // SUBS, lax.rem(v, SUBS)
+            d = jnp.where(way == 0, NZ - 1 - s, s)
+            joined = (k == 0) & second & (s > 0)
+
+            @pl.when(q == 0)
+            def _():
+                wait_tokens(d)
+
+            acc[...] = multiply(tokg[d], cotg[q])
+
+            @pl.when(joined)
+            def _():
+                @pl.when(q == 0)
+                def _():
+                    edge_tokens(s).wait_recv()
+
+                @pl.when(s == 1)
+                def _():
+                    for peer in (1, 2, 3):
+                        edge_relay(q, peer).wait_recv()
+
+                acc[...] += multiply(tok_edge[s - 1], cot_edge[q])
+
+            @pl.when(jnp.logical_not(joined | (edge & (k == 0))))
+            def _():
+                stream(way, v).wait_recv()
+                acc[...] += buf[way, s, q].astype(F32)
+
+            buf[way, s, q] = acc[...].astype(BF16)
+
+            @pl.when(v >= DEPTH)
+            def _():
+                stream(way, v - DEPTH).wait_send()
+
+            stream(way, v).start()
+
+    def forward_tokens(u):
+        s = (u - 4) // 2 + 1
+
+        @pl.when(edge & (u >= 4) & (u <= 14) & (lax.rem(u, 2) == 0))
+        def _():
+            wait_tokens(dest(s))
+
+            @pl.when(s >= 3)
+            def _():
+                edge_tokens(s - 2).wait_send()
+
+            edge_tokens(s).start()
 
     def step(u, _):
         @pl.when(u < SUBS)
@@ -278,22 +391,18 @@
             for k in (1, 2, 3):
                 cot_copy(u, k).wait_recv()
 
-        uf = u - lag_f
-        ub = u - lag_b
-
-        @pl.when((uf >= 0) & (uf < count_f))
-        def _():
-            unit(uf, NZ - 1 - uf // SUBS, z == 0, buf_f, forward)
-
-        @pl.when((ub >= 0) & (ub < count_b))
-        def _():
-            unit(ub, ub // SUBS, z == NZ - 1, buf_b, backward)
+        def both(k, _):
+            unit(k, u)
+            return 0
+
+        lax.fori_loop(0, 2, both, 0)
+        forward_tokens(u)
 
         @pl.when(u < NZ - 2)
         def _():
-            send_tokens(order(u + 2))
-
-        for at, stage in stages.items():
+            send_tokens(dest(order(u + 2)))
+
+        for at, stage in stages:
             pl.when(u == at)(stage)
         return 0
 
@@ -315,23 +424,39 @@
     ]
     tall = jnp.concatenate(tall, axis=0)
     rate = tall[:, :1] * (mix_weight * inner_gain / math.sqrt(32 * 128))
-    for q in range(SUBS):
-        full_sum = product(z, q)
-        half_w = mix_weight * w[:, q * COLS : (q + 1) * COLS].astype(F32) + (1.0 - mix_weight) * sh[q].astype(F32)
-
-        @pl.when(z > 0)
-        def _():
-            forward((NZ - 1 - z) * SUBS + q).wait_recv()
-
-        @pl.when(z < NZ - 1)
-        def _():
-            backward(z * SUBS + q).wait_recv()
-
-        near_f = jnp.minimum(NZ - 1 - z, NZ - 2)
-        near_b = jnp.minimum(z, NZ - 2)
-        left = jnp.where(z > 0, buf_f[near_f, q].astype(F32), 0.0)
-        right = jnp.where(z < NZ - 1, buf_b[near_b, q].astype(F32), 0.0)
-        layer_out[:, q * COLS : (q + 1) * COLS] = (half_w - rate * (full_sum + left + right)).astype(BF16)
+
+    def layer_store(q):
+        at = pl.ds(pl.multiple_of(q * COLS, COLS), COLS)
+        return pltpu.make_async_copy(layer.at[:, at], layer_out.at[:, at], out_sem.at[2 + q])
+
+    @pl.when(second)
+    def _():
+        edge_tokens(NZ - 2).wait_recv()
+
+    def finish(q, _):
+        at = pl.ds(pl.multiple_of(q * COLS, COLS), COLS)
+        acc[...] = multiply(tokg[z], cotg[q])
+
+        @pl.when(second)
+        def _():
+            acc[...] += multiply(tok_edge[NZ - 3], cot_edge[q])
+
+        @pl.when(z > 1)
+        def _():
+            stream(0, (NZ - 1 - z) * SUBS + q).wait_recv()
+            acc[...] += buf[0, NZ - 1 - z, q].astype(F32)
+
+        @pl.when(z < NZ - 2)
+        def _():
+            stream(1, z * SUBS + q).wait_recv()
+            acc[...] += buf[1, z, q].astype(F32)
+
+        half_w = mix_weight * w[:, at].astype(F32) + (1.0 - mix_weight) * sh[q].astype(F32)
+        layer[:, at] = (half_w - rate * acc[...]).astype(BF16)
+        layer_store(q).start()
+        return 0
+
+    lax.fori_loop(0, SUBS, finish, 0)
 
     for k in (1, 2, 3):
         for d in range(NZ):
@@ -343,15 +468,34 @@
     for copy in (core_sum, z_sum, core_full, core_pair, z_gather, core_gather):
         copy.wait_send()
 
-    @pl.when(z < NZ - 1)
-    def _():
-        for back in range(DEPTH):
-            forward(count_f - 1 - back).wait_send()
-
-    @pl.when(z > 0)
-    def _():
-        for back in range(DEPTH):
-            backward(count_b - 1 - back).wait_send()
+    for store in stores + [layer_store(q) for q in range(SUBS)]:
+        store.wait()
+
+    for back in range(1, DEPTH + 1):
+        stream(inner, count_in - back).wait_send()
+
+    @pl.when(depth > 0)
+    def _():
+        for back in range(1, DEPTH + 1):
+            stream(1 - inner, count_out - back).wait_send()
+
+    @pl.when(edge)
+    def _():
+        for q in range(SUBS):
+            edge_cot(q).wait_send()
+        for s in (NZ - 3, NZ - 2):
+            edge_tokens(s).wait_send()
+
+    @pl.when(second)
+    def _():
+        for q in range(SUBS):
+            for k in (1, 2, 3):
+                edge_relay(q, k).wait_send()
+
+
+def copy_kernel(*refs):
+    for a, b in zip(refs[:3], refs[3:]):
+        b[...] = a[...]
 
 
 def on_device(tokens, norm_gain, cotangent, layer_weight, shared_copy, master, momentum):
@@ -359,38 +503,51 @@
     dma = pltpu.SemaphoreType.DMA
     scratch = [
         vmem((128, 8192), BF16), vmem((128, 1024), BF16), vmem((256, 1024), BF16), vmem((256, 1024), BF16),
-        vmem((256, 64), F32), vmem((256, 64), F32),
+        vmem((64, 256), F32), vmem((64, 256), F32),
+        vmem((256, 1024), BF16), vmem((64, 256), F32), vmem((64, 256), F32),
         vmem((NZ, 512, COLS), BF16), vmem((SUBS, 512, COLS), BF16),
-        vmem((NZ - 1, SUBS, 256, COLS), BF16), vmem((NZ - 1, SUBS, 256, COLS), BF16),
+        vmem((2, NZ - 1, SUBS, 256, COLS), BF16), vmem((256, COLS), F32),
+        vmem((NZ - 2, 512, COLS), BF16), vmem((SUBS, 512, COLS), BF16),
         vmem((4, 256, 256), BF16), vmem((3, 256, 256), BF16), vmem((128, 256), F32),
         vmem((128, 256), BF16), vmem((128, 256), BF16), vmem((128, 128), BF16), vmem((128, 128), BF16),
         vmem((256, 128), F32), vmem((256, 128), BF16), vmem((256, 128), BF16),
         vmem((4, 256, 256), BF16), vmem((4, 128, 256), BF16),
         dma((6,)),
         dma((NZ, 3)), dma((NZ, 3)), dma((SUBS, 3)), dma((SUBS, 3)),
-        dma((UNITS,)), dma((UNITS,)), dma((UNITS,)), dma((UNITS,)),
+        dma((2, UNITS)), dma((2, UNITS)),
+        dma((NZ - 2,)), dma((NZ - 2,)), dma((SUBS,)), dma((SUBS,)), dma((SUBS, 3)), dma((SUBS, 3)),
         dma((3,)), dma((3,)), dma((3,)), dma((3,)), dma((6,)), dma((6,)),
+        dma((6,)), pltpu.SemaphoreType.REGULAR, pltpu.SemaphoreType.REGULAR,
     ]
     layer_next, master_next, momentum_next = pl.pallas_call(
         kernel,
         out_shape=[
             jax.ShapeDtypeStruct((256, 1024), BF16),
-            jax.ShapeDtypeStruct((256, 64), F32),
-            jax.ShapeDtypeStruct((256, 64), F32),
+            jax.ShapeDtypeStruct((64, 256), F32),
+            jax.ShapeDtypeStruct((64, 256), F32),
         ],
         in_specs=[pl.BlockSpec(memory_space=hbm), pl.BlockSpec(memory_space=vmem)]
         + [pl.BlockSpec(memory_space=hbm)] * 5,
-        out_specs=[pl.BlockSpec(memory_space=vmem)] * 3,
+        out_specs=[pl.BlockSpec(memory_space=hbm)] * 3,
         scratch_shapes=scratch,
         name="diloco_step",
         cost_estimate=pl.CostEstimate(flops=2 * 4096 * 256 * 1024, bytes_accessed=5 << 20, transcendentals=0),
         compiler_params=pltpu.CompilerParams(
-            collective_id=0, has_side_effects=True, vmem_limit_bytes=48 << 20
+            collective_id=0, has_side_effects=True, vmem_limit_bytes=60 << 20
         ),
     )(
-        tokens[0], norm_gain.reshape(64, 128), cotangent[0], layer_weight[0], shared_copy, master, momentum
+        tokens[0], norm_gain.reshape(64, 128), cotangent[0], layer_weight[0], shared_copy, master.T, momentum.T
     )
-    return (layer_next[None], master_next, momentum_next)
+    results = (layer_next, master_next, momentum_next)
+    layer_next, master_next, momentum_next = pl.pallas_call(
+        copy_kernel,
+        out_shape=[jax.ShapeDtypeStruct(r.shape, r.dtype) for r in results],
+        in_specs=[pl.BlockSpec(memory_space=vmem)] * 3,
+        out_specs=[pl.BlockSpec(memory_space=vmem)] * 3,
+        name="write_out",
+        compiler_params=pltpu.CompilerParams(vmem_limit_bytes=60 << 20),
+    )(*results)
+    return (layer_next[None], master_next.T, momentum_next.T)
 
 
 def solution(mesh):

time: 123 us -> 104 us (0.85)
  the two profiles are of different devices: /device:TPU:6 before, /device:TPU:161 now
where the time goes in v2:
time: 104 us
  Pallas kernels  103 us (99%)
    pallas_call x1, Pallas kernels, on_device(): pl.pallas_call(kernel, out_shape=[jax.ShapeDtypeStruct((256, 1024), BF16)...  101 us

profile of v2, /device:TPU:161, one launch (start us, length us, event | category | flops | bytes accessed | tf_op | source)
XLA Modules:
  0.0 104.0 jit_solution(15151947861306328123)
XLA Ops:
  0.6 101.4 %diloco_step.1 = (bf16[256,1024]{1,0:T(8,128)(2,1)}, f32[64,256]{1,0:T(8,128)}, f32[64,256]{1,0:T(8,128)}) custom-call(bf16[128,8192]{1,0:T(8,128)(2,1)} %bitcast.9, bf16[64,128]{1,0:T(8,128)(2,1)} %bitcast.17, bf16[128,1024]{1,0:T(8,128)(2,1)} %bitcast.12, bf16[256,1024]{1,0:T(8,128)(2,1)} %bitcast.10, bf16[256,1024]{1,0:T(8,128)(2,1)} %shared_hbm.1, ...), custom_call_target="tpu_custom_call" | custom-call | flops 2147483648 | bytes 5242880 | tf_op jit(solution)/shard_map/diloco_step/pallas_call | solution.py:522
  102.0 1.9 %write_out.1 = (bf16[256,1024]{1,0:T(8,128)(2,1)}, f32[64,256]{1,0:T(8,128)}, f32[64,256]{1,0:T(8,128)}) custom-call(bf16[256,1024]{1,0:T(8,128)(2,1)} %get-tuple-element.9.refs_0_, f32[64,256]{1,0:T(8,128)} %get-tuple-element.10.refs_1_, f32[64,256]{1,0:T(8,128)} %get-tuple-element.11.refs_2_), custom_call_target="tpu_custom_call" | custom-call | tf_op jit(solution)/shard_map/write_out/pallas_call | solution.py:542

commit v3 on v2

--- a/solution.py
+++ b/solution.py
@@ -22,15 +22,16 @@
 F32, BF16 = jnp.float32, jnp.bfloat16
 COLS = 256
 SUBS = 4
-UNITS = (NZ - 1) * SUBS
-DEPTH = 3
+PARTS = 2 * SUBS
+UNITS = (NZ - 1) * PARTS
+DEPTH = 4
 
 
 def kernel(
     tok_hbm, gain_ref, cot_hbm, w_hbm, shared_hbm, master_hbm, mom_hbm,
     layer_out, master_out, mom_out,
     tok, cot, w, shared, master, mom, layer, master_new, mom_new,
-    tokg, cotg, buf, acc, tok_edge, cot_edge, dec, x_in, half, core_out, core_in, z_out, z_in,
+    tokg, cotg, buf, acc, own, rates, tok_edge, cot_edge, dec, x_in, half, core_out, core_in, z_out, z_in,
     full, pair_out, pair_in, sh, sh_in,
     load_sem, st, rt, sc, rc, su, ru, ste, rte, sce, rce, sye, rye, sx, rx, sg, rg, ss, rs, out_sem, wave_up, wave_down,
 ):
@@ -100,28 +101,49 @@
     def columns_of(peer, d):
         return pl.ds(pl.multiple_of((peer * NZ + d) * COLS, COLS), COLS)
 
+    def half_columns(peer, d, h):
+        return pl.ds(pl.multiple_of((peer * NZ + d) * COLS + h * 128, 128), 128)
+
     def token_copy(d, k):
         peer = y_peer(k)
+        return remote(tok.at[:, columns_of(peer, d)], tokg.at[d, my_rows()], st, rt.at[d], device(y=peer))
+
+    def token_half(d, k, h):
+        peer = y_peer(k)
         return remote(
-            tok.at[:, columns_of(peer, d)], tokg.at[d, my_rows()], st.at[d, k - 1], rt.at[d, k - 1], device(y=peer)
+            tok.at[:, half_columns(peer, d, h)], tokg.at[d, my_rows(), pl.ds(h * 128, 128)],
+            st, rt.at[d if h == 0 else NZ], device(y=peer),
         )
 
     def cot_copy(q, k):
-        return remote(
-            cotg.at[q, my_rows()], cotg.at[q, my_rows()], sc.at[q, k - 1], rc.at[q, k - 1], device(y=y_peer(k))
-        )
+        return remote(cotg.at[q, my_rows()], cotg.at[q, my_rows()], sc, rc.at[q], device(y=y_peer(k)))
+
+    def arrived(ref, sem):
+        remote(ref, ref, st, sem, device(y=y_peer(1))).wait_recv()
+
+    def departed(ref, sem):
+        remote(ref, ref, sem, rt.at[0], device(y=y_peer(1))).wait_send()
+
+    three = pl.ds(0, 3 * 128)
+
+    def wait_half(h):
+        d = dest(0)
+        arrived(tokg.at[d, three, pl.ds(h * 128, 128)], rt.at[d if h == 0 else NZ])
 
     def send_tokens(d):
         for k in (1, 2, 3):
             token_copy(d, k).start()
 
     def wait_tokens(d):
-        for k in (1, 2, 3):
-            token_copy(d, k).wait_recv()
+        arrived(tokg.at[d, three], rt.at[d])
+
+    def wait_cots(q):
+        arrived(cotg.at[q, three], rc.at[q])
 
     loads[0].wait()
     pl.semaphore_wait(barrier, 7 + jnp.where(line > 0, 1, 0) + jnp.where(line < last, 1, 0))
-    send_tokens(dest(0))
+    for k in (1, 2, 3):
+        token_half(dest(0), k, 0).start()
     for load in loads[2:]:
         load.start()
 
@@ -136,21 +158,27 @@
         cotg[q, my_rows(), :] = (cot[:, q * COLS : (q + 1) * COLS].astype(F32) * inverse).astype(BF16)
         for k in (1, 2, 3):
             cot_copy(q, k).start()
-    send_tokens(dest(1))
+        if q == 0:
+            for k in (1, 2, 3):
+                token_half(dest(0), k, 1).start()
 
     def edge_cot(q):
         return remote(
-            cotg.at[q, my_rows()], cot_edge.at[q, my_rows()], sce.at[q], rce.at[q], device(z=inward)
+            cotg.at[q, my_rows()], cot_edge.at[q, my_rows()], sce, rce, device(z=inward)
         )
 
     def edge_relay(q, k):
         return remote(
-            cot_edge.at[q, my_rows()], cot_edge.at[q, my_rows()], sye.at[q, k - 1], rye.at[q, k - 1],
+            cot_edge.at[q, my_rows()], cot_edge.at[q, my_rows()], sye, rye.at[q],
             device(y=y_peer(k)),
         )
 
-    def edge_tokens(s):
-        return remote(tokg.at[dest(s)], tok_edge.at[s - 1], ste.at[s - 1], rte.at[s - 1], device(z=inward))
+    def edge_tokens(s, h):
+        lanes = pl.ds(h * 128, 128)
+        return remote(
+            tokg.at[dest(s), :, lanes], tok_edge.at[s - 1, :, lanes],
+            ste.at[lax.rem(s, 2)], rte.at[s - 1, h], device(z=inward),
+        )
 
     @pl.when(edge)
     def _():
@@ -201,20 +229,13 @@
 
     def scatter_copy(k):
         peer = x_peer(k)
-        return remote(dec.at[peer], x_in.at[k - 1], sx.at[k - 1], rx.at[k - 1], device(x=peer))
+        return remote(dec.at[peer], x_in.at[k - 1], sx, rx, device(x=peer))
 
     for k in (1, 2, 3):
         scatter_copy(k).start()
 
     near_half = zh == 0
     pl.when(near_half)(pass_up)
-
-    @pl.when(second)
-    def _():
-        for q in range(SUBS):
-            edge_cot(q).wait_recv()
-            for k in (1, 2, 3):
-                edge_relay(q, k).start()
 
     mine = pl.ds(pl.multiple_of(c * 128, 128), 128)
     other = pl.ds(pl.multiple_of((1 - c) * 128, 128), 128)
@@ -222,15 +243,15 @@
     far_lanes = pl.ds(pl.multiple_of((1 - zh) * 128, 128), 128)
     core = device(c=1 - c)
     far = device(zh=1 - zh)
-    core_sum = remote(core_out, core_in, ss.at[0], rs.at[0], core)
-    z_sum = remote(z_out, z_in, ss.at[1], rs.at[1], far)
-    core_full = remote(full.at[mine], full.at[mine], ss.at[2], rs.at[2], core)
-    core_pair = remote(pair_out, pair_in, ss.at[3], rs.at[3], core)
-    z_gather = remote(sh.at[x, mine, my_lanes], sh.at[x, mine, my_lanes], ss.at[4], rs.at[4], far)
-    core_gather = remote(sh.at[:, mine], sh_in, ss.at[5], rs.at[5], core)
+    core_sum = remote(core_out, core_in, ss, rs.at[0], core)
+    z_sum = remote(z_out, z_in, ss, rs.at[1], far)
+    core_full = remote(full.at[mine], full.at[mine], ss, rs.at[2], core)
+    core_pair = remote(pair_out, pair_in, ss, rs.at[3], core)
+    z_gather = remote(sh.at[x, mine, my_lanes], sh.at[x, mine, my_lanes], ss, rs.at[4], far)
+    core_gather = remote(sh.at[:, mine], sh_in, ss, rs.at[5], core)
 
     def gather_copy(k):
-        return remote(sh.at[x, mine], sh.at[x, mine], sg.at[k - 1], rg.at[k - 1], device(x=x_peer(k)))
+        return remote(sh.at[x, mine], sh.at[x, mine], sg, rg, device(x=x_peer(k)))
 
     stores = [
         pltpu.make_async_copy(src, dst, out_sem.at[i])
@@ -238,8 +259,7 @@
     ]
 
     def stage_x():
-        for k in (1, 2, 3):
-            scatter_copy(k).wait_recv()
+        arrived(x_in, rx)
 
         def summed(rows):
             acc = dec[x, rows, :].astype(F32)
@@ -290,8 +310,7 @@
             gather_copy(k).start()
 
     def stage_last():
-        for k in (1, 2, 3):
-            gather_copy(k).wait_recv()
+        arrived(sh_in.at[pl.ds(0, 3)], rg)
         core_gather.start()
 
     def pick(*choices):
@@ -300,71 +319,96 @@
             at = jnp.where(depth == i, choices[i], at)
         return at
 
-    up_at = jnp.where(z < 5, 0, jnp.where(z == 5, 2, jnp.where(z == 6, 4, 9)))
-    down_far = jnp.where(z > 2, 0, jnp.where(z == 2, 2, jnp.where(z == 1, 4, 9)))
-    down_near = jnp.where(low_half, pick(14, 9, 7, 5), pick(10, 6, 5, 4))
-    core_at = jnp.where(near_half, down_near, jnp.maximum(up_at, 2))
-    far_at = pick(15, 11, 10, 9)
-    gather_at = jnp.where(near_half, pick(21, 21, 20, 19), pick(19, 16, 16, 16))
+    def by_place(low, high):
+        return jnp.where(low_half, pick(*low), pick(*high))
+
+    up_at = by_place((1, 1, 1, 1), (10, 8, 4, 1))
+    down_far = by_place((10, 8, 4, 1), (1, 1, 1, 1))
+    down_near = by_place((22, 20, 16, 10), (12, 12, 10, 8))
+    core_at = jnp.where(near_half, down_near, jnp.maximum(up_at, 4))
+    far_at = jnp.where(
+        near_half, by_place((24, 23, 20, 18), (18, 18, 16, 16)), by_place((24, 23, 20, 17), (20, 20, 18, 17))
+    )
+    gather_at = jnp.where(near_half, by_place((42, 42, 38, 35), (36, 35, 34, 34)), pick(32, 32, 30, 29))
     stages = [
-        (1, stage_x),
+        (2, stage_x),
         (up_at, lambda: pl.when(jnp.logical_not(near_half))(pass_up)),
         (jnp.where(near_half, down_near, down_far), pass_down),
         (core_at, stage_core),
         (far_at, stage_far),
-        (far_at + 1, stage_update),
-        (far_at + 2, stage_pair),
+        (far_at + 2, stage_update),
+        (far_at + 4, stage_pair),
         (gather_at, stage_gather),
-        (gather_at + 2, stage_last),
+        (gather_at + 4, stage_last),
     ]
 
-    def multiply(rows, q):
-        return lax.dot_general(rows, q, (((0,), (0,)), ((), ())), preferred_element_type=F32)
-
-    def stream(way, u):
-        s, q = u // SUBS, lax.rem(u, SUBS)
+    def multiply(rows, columns):
+        return lax.dot_general(rows, columns, (((0,), (0,)), ((), ())), preferred_element_type=F32)
+
+    def split(j, by_column):
+        h = jnp.where(by_column, lax.rem(j, 2), lax.rem(j // 2, 2))
+        q = jnp.where(by_column, j // 2, 2 * (j // SUBS) + lax.rem(j, 2))
+        return pl.ds(pl.multiple_of(h * 128, 128), 128), q
+
+    def stream(way, v):
+        s, j = v // PARTS, lax.rem(v, PARTS)
         to = jnp.where(way == 0, z + 1, z - 1)
-        return remote(buf.at[way, s, q], buf.at[way, s, q], su.at[way, u], ru.at[way, u], device(z=to))
-
-    count_in = jnp.where(edge, SUBS, SUBS * (NZ - 1 - depth))
-    count_out = SUBS * depth
+        slot = jnp.where(way == 0, v, NZ * PARTS + PARTS - 1 - v)
+        return remote(
+            buf.at[way, s, j], buf.at[way, s, j], su.at[way, lax.rem(v, DEPTH)], ru.at[slot], device(z=to)
+        )
+
+    count_in = jnp.where(edge, PARTS, PARTS * (NZ - 1 - depth))
+    count_out = PARTS * depth
     inner = jnp.where(low_half, 0, 1)
+
+    def wait_first(k, d, h):
+        @pl.when(k == 0)
+        def _():
+            wait_half(h)
+
+        if h == 0:
+            pl.when(k == 1)(lambda: wait_tokens(d))
 
     def unit(k, u):
         way = jnp.where(k == 0, inner, 1 - inner)
-        v = jnp.where(k == 0, u, u - (18 - 4 * depth))
+        v = jnp.where(k == 0, u, u - (36 - 8 * depth))
 
         @pl.when((v >= 0) & (v < jnp.where(k == 0, count_in, count_out)))
         def _():
-            s, q = v // SUBS, lax.rem(v, SUBS)
+            s, j = v // PARTS, lax.rem(v, PARTS)
             d = jnp.where(way == 0, NZ - 1 - s, s)
+            rows, q = split(j, s == 0)
             joined = (k == 0) & second & (s > 0)
 
-            @pl.when(q == 0)
+            @pl.when(s == 0)
+            def _():
+                for h in range(2):
+                    pl.when(j == h)(lambda: wait_first(k, d, h))
+
+            @pl.when((s > 0) & (j == 0))
             def _():
                 wait_tokens(d)
 
-            acc[...] = multiply(tokg[d], cotg[q])
+            acc[...] = multiply(tokg[d, :, rows], cotg[q])
 
             @pl.when(joined)
             def _():
-                @pl.when(q == 0)
+                for h in range(2):
+                    pl.when(j == 2 * h)(lambda: edge_tokens(s, h).wait_recv())
+
+                @pl.when((s == 1) & (lax.rem(j // 2, 2) == 0))
                 def _():
-                    edge_tokens(s).wait_recv()
-
-                @pl.when(s == 1)
-                def _():
-                    for peer in (1, 2, 3):
-                        edge_relay(q, peer).wait_recv()
-
-                acc[...] += multiply(tok_edge[s - 1], cot_edge[q])
+                    arrived(cot_edge.at[q, three], rye.at[q])
+
+                acc[...] += multiply(tok_edge[s - 1, :, rows], cot_edge[q])
 
             @pl.when(jnp.logical_not(joined | (edge & (k == 0))))
             def _():
                 stream(way, v).wait_recv()
-                acc[...] += buf[way, s, q].astype(F32)
-
-            buf[way, s, q] = acc[...].astype(BF16)
+                acc[...] += buf[way, s, j].astype(F32)
+
+            buf[way, s, j] = acc[...].astype(BF16)
 
             @pl.when(v >= DEPTH)
             def _():
@@ -373,23 +417,40 @@
             stream(way, v).start()
 
     def forward_tokens(u):
-        s = (u - 4) // 2 + 1
-
-        @pl.when(edge & (u >= 4) & (u <= 14) & (lax.rem(u, 2) == 0))
+        s = (u - PARTS) // 4 + 1
+
+        @pl.when(edge & (u >= PARTS) & (s < NZ - 1) & (lax.rem(u, 4) == 0))
         def _():
             wait_tokens(dest(s))
 
             @pl.when(s >= 3)
             def _():
-                edge_tokens(s - 2).wait_send()
-
-            edge_tokens(s).start()
+                departed(tokg.at[0], ste.at[lax.rem(s, 2)])
+
+            for h in range(2):
+                edge_tokens(s, h).start()
+
+    relays = jnp.where(second, SUBS, 0)
+
+    def y_job(u):
+        i = u // 2
+
+        @pl.when((lax.rem(u, 2) == 0) & (i <= NZ - 2 + relays))
+        def _():
+            pl.when(i == 0)(lambda: send_tokens(dest(1)))
+
+            @pl.when((i > 0) & (i <= relays))
+            def _():
+                pl.when(i == 1)(lambda: arrived(cot_edge.at[:, my_rows()], rce))
+                for k in (1, 2, 3):
+                    edge_relay(i - 1, k).start()
+
+            pl.when(i > relays)(lambda: send_tokens(dest(order(i - relays + 1))))
 
     def step(u, _):
-        @pl.when(u < SUBS)
-        def _():
-            for k in (1, 2, 3):
-                cot_copy(u, k).wait_recv()
+        @pl.when((u < PARTS) & (lax.rem(u, 2) == 0))
+        def _():
+            wait_cots(u // 2)
 
         def both(k, _):
             unit(k, u)
@@ -398,10 +459,7 @@
         lax.fori_loop(0, 2, both, 0)
         forward_tokens(u)
 
-        @pl.when(u < NZ - 2)
-        def _():
-            send_tokens(dest(order(u + 2)))
-
+        y_job(u)
         for at, stage in stages:
             pl.when(u == at)(stage)
         return 0
@@ -409,67 +467,64 @@
     lax.fori_loop(0, UNITS, step, 0)
 
     wait_tokens(z)
+
+    @pl.when(second)
+    def _():
+        for h in range(2):
+            edge_tokens(NZ - 2, h).wait_recv()
+
     core_gather.wait_recv()
     for q in range(SUBS):
         sh[q, other, :] = sh_in[q]
     row = lax.broadcasted_iota(jnp.int32, (64, 128), 0)
-    gain = gain_ref[...].astype(F32)
-    tall = [
-        jnp.transpose(
-            jnp.broadcast_to(
-                jnp.sum(jnp.where(row == 2 * fs + h, gain, 0.0), axis=0, keepdims=True), (128, 128)
-            )
-        )
-        for h in range(2)
-    ]
-    tall = jnp.concatenate(tall, axis=0)
-    rate = tall[:, :1] * (mix_weight * inner_gain / math.sqrt(32 * 128))
-
-    def layer_store(q):
+    gain = gain_ref[...].astype(F32) * (mix_weight * inner_gain / math.sqrt(32 * 128))
+    for h in range(2):
+        line_gain = jnp.sum(jnp.where(row == 2 * fs + h, gain, 0.0), axis=0, keepdims=True)
+        tall = jnp.transpose(jnp.broadcast_to(line_gain, (128, 128)))
+        rates[pl.ds(h * 128, 128), :] = jnp.concatenate([tall, tall], axis=1)
+
+    def prepare(j, _):
+        rows, q = split(j, edge)
         at = pl.ds(pl.multiple_of(q * COLS, COLS), COLS)
-        return pltpu.make_async_copy(layer.at[:, at], layer_out.at[:, at], out_sem.at[2 + q])
-
-    @pl.when(second)
-    def _():
-        edge_tokens(NZ - 2).wait_recv()
-
-    def finish(q, _):
+        acc[...] = multiply(tokg[z, :, rows], cotg[q])
+
+        @pl.when(second)
+        def _():
+            acc[...] += multiply(tok_edge[NZ - 3, :, rows], cot_edge[q])
+
+        half_w = mix_weight * w[rows, at].astype(F32) + (1.0 - mix_weight) * sh[q, rows, :].astype(F32)
+        own[j] = half_w - rates[rows, :] * acc[...]
+        return 0
+
+    lax.fori_loop(0, PARTS, prepare, 0)
+
+    def finish(j, _):
+        rows, q = split(j, edge)
         at = pl.ds(pl.multiple_of(q * COLS, COLS), COLS)
-        acc[...] = multiply(tokg[z], cotg[q])
-
-        @pl.when(second)
-        def _():
-            acc[...] += multiply(tok_edge[NZ - 3], cot_edge[q])
 
         @pl.when(z > 1)
         def _():
-            stream(0, (NZ - 1 - z) * SUBS + q).wait_recv()
-            acc[...] += buf[0, NZ - 1 - z, q].astype(F32)
+            stream(0, (NZ - 1 - z) * PARTS + j).wait_recv()
+            own[j] -= rates[rows, :] * buf[0, NZ - 1 - z, j].astype(F32)
 
         @pl.when(z < NZ - 2)
         def _():
-            stream(1, z * SUBS + q).wait_recv()
-            acc[...] += buf[1, z, q].astype(F32)
-
-        half_w = mix_weight * w[:, at].astype(F32) + (1.0 - mix_weight) * sh[q].astype(F32)
-        layer[:, at] = (half_w - rate * acc[...]).astype(BF16)
-        layer_store(q).start()
+            stream(1, z * PARTS + j).wait_recv()
+            own[j] -= rates[rows, :] * buf[1, z, j].astype(F32)
+
+        layer[rows, at] = own[j].astype(BF16)
+        pltpu.make_async_copy(layer.at[rows, at], layer_out.at[rows, at], out_sem.at[2]).start()
         return 0
 
-    lax.fori_loop(0, SUBS, finish, 0)
-
-    for k in (1, 2, 3):
-        for d in range(NZ):
-            token_copy(d, k).wait_send()
-        for q in range(SUBS):
-            cot_copy(q, k).wait_send()
-        scatter_copy(k).wait_send()
-        gather_copy(k).wait_send()
-    for copy in (core_sum, z_sum, core_full, core_pair, z_gather, core_gather):
-        copy.wait_send()
-
-    for store in stores + [layer_store(q) for q in range(SUBS)]:
+    lax.fori_loop(0, PARTS, finish, 0)
+    departed(tok.at[:, pl.ds(0, 6144)], st)
+    departed(cotg.at[pl.ds(0, 3)], sc)
+    departed(dec.at[pl.ds(0, 3)], sx)
+    departed(sh_in.at[pl.ds(0, 3)], sg)
+    departed(dec, ss)
+    for store in stores:
         store.wait()
+    pltpu.make_async_copy(layer, layer_out, out_sem.at[2]).wait()
 
     for back in range(1, DEPTH + 1):
         stream(inner, count_in - back).wait_send()
@@ -481,16 +536,13 @@
 
     @pl.when(edge)
     def _():
-        for q in range(SUBS):
-            edge_cot(q).wait_send()
-        for s in (NZ - 3, NZ - 2):
-            edge_tokens(s).wait_send()
+        departed(cotg.at[0], sce)
+        for s in range(2):
+            departed(tokg.at[0], ste.at[s])
 
     @pl.when(second)
     def _():
-        for q in range(SUBS):
-            for k in (1, 2, 3):
-                edge_relay(q, k).wait_send()
+        departed(cot_edge.at[pl.ds(0, 3)], sye)
 
 
 def copy_kernel(*refs):
@@ -506,18 +558,18 @@
         vmem((64, 256), F32), vmem((64, 256), F32),
         vmem((256, 1024), BF16), vmem((64, 256), F32), vmem((64, 256), F32),
         vmem((NZ, 512, COLS), BF16), vmem((SUBS, 512, COLS), BF16),
-        vmem((2, NZ - 1, SUBS, 256, COLS), BF16), vmem((256, COLS), F32),
+        vmem((2, NZ - 1, PARTS, 128, COLS), BF16), vmem((128, COLS), F32),
+        vmem((PARTS, 128, COLS), F32), vmem((256, COLS), F32),
         vmem((NZ - 2, 512, COLS), BF16), vmem((SUBS, 512, COLS), BF16),
         vmem((4, 256, 256), BF16), vmem((3, 256, 256), BF16), vmem((128, 256), F32),
         vmem((128, 256), BF16), vmem((128, 256), BF16), vmem((128, 128), BF16), vmem((128, 128), BF16),
         vmem((256, 128), F32), vmem((256, 128), BF16), vmem((256, 128), BF16),
         vmem((4, 256, 256), BF16), vmem((4, 128, 256), BF16),
-        dma((6,)),
-        dma((NZ, 3)), dma((NZ, 3)), dma((SUBS, 3)), dma((SUBS, 3)),
-        dma((2, UNITS)), dma((2, UNITS)),
-        dma((NZ - 2,)), dma((NZ - 2,)), dma((SUBS,)), dma((SUBS,)), dma((SUBS, 3)), dma((SUBS, 3)),
-        dma((3,)), dma((3,)), dma((3,)), dma((3,)), dma((6,)), dma((6,)),
-        dma((6,)), pltpu.SemaphoreType.REGULAR, pltpu.SemaphoreType.REGULAR,
+        dma((6,)), dma, dma((NZ + 1,)), dma, dma((SUBS,)),
+        dma((2, DEPTH)), dma(((NZ + 1) * PARTS,)),
+        dma((2,)), dma((NZ - 2, 2)), dma, dma, dma, dma((SUBS,)),
+        dma, dma, dma, dma, dma, dma((6,)), dma((3,)),
+        pltpu.SemaphoreType.REGULAR, pltpu.SemaphoreType.REGULAR,
     ]
     layer_next, master_next, momentum_next = pl.pallas_call(
         kernel,

time: 104 us -> 100 us (0.962)
  the two profiles are of different devices: /device:TPU:161 before, /device:TPU:160 now
where the time goes in v3:
time: 100 us; the launch traced here: 99.9 us
  Pallas kernels  99.3 us (99%)
    pallas_call x1, Pallas kernels, on_device(): pl.pallas_call(kernel, out_shape=[jax.ShapeDtypeStruct((256, 1024), BF16)...  97.4 us

profile of v3, /device:TPU:160, one launch (start us, length us, event | category | flops | bytes accessed | tf_op | source)
XLA Modules:
  0.0 99.9 jit_solution(8093564086782187881)
XLA Ops:
  0.6 97.4 %diloco_step.1 = (bf16[256,1024]{1,0:T(8,128)(2,1)}, f32[64,256]{1,0:T(8,128)}, f32[64,256]{1,0:T(8,128)}) custom-call(bf16[128,8192]{1,0:T(8,128)(2,1)} %bitcast.9, bf16[64,128]{1,0:T(8,128)(2,1)} %bitcast.17, bf16[128,1024]{1,0:T(8,128)(2,1)} %bitcast.12, bf16[256,1024]{1,0:T(8,128)(2,1)} %bitcast.10, bf16[256,1024]{1,0:T(8,128)(2,1)} %shared_hbm.1, ...), custom_call_target="tpu_custom_call" | custom-call | flops 2147483648 | bytes 5242880 | tf_op jit(solution)/shard_map/diloco_step/pallas_call | solution.py:574
  98.0 1.9 %write_out.1 = (bf16[256,1024]{1,0:T(8,128)(2,1)}, f32[64,256]{1,0:T(8,128)}, f32[64,256]{1,0:T(8,128)}) custom-call(bf16[256,1024]{1,0:T(8,128)(2,1)} %get-tuple-element.9.refs_0_, f32[64,256]{1,0:T(8,128)} %get-tuple-element.10.refs_1_, f32[64,256]{1,0:T(8,128)} %get-tuple-element.11.refs_2_), custom_call_target="tpu_custom_call" | custom-call | tf_op jit(solution)/shard_map/write_out/pallas_call | solution.py:594

commit v4 on v3

--- a/solution.py
+++ b/solution.py
@@ -24,7 +24,7 @@
 SUBS = 4
 PARTS = 2 * SUBS
 UNITS = (NZ - 1) * PARTS
-DEPTH = 4
+DEPTH = 8
 
 
 def kernel(
@@ -156,9 +156,9 @@
     loads[1].wait()
     for q in range(SUBS):
         cotg[q, my_rows(), :] = (cot[:, q * COLS : (q + 1) * COLS].astype(F32) * inverse).astype(BF16)
-        for k in (1, 2, 3):
-            cot_copy(q, k).start()
         if q == 0:
+            for k in (1, 2, 3):
+                cot_copy(q, k).start()
             for k in (1, 2, 3):
                 token_half(dest(0), k, 1).start()
 
@@ -236,6 +236,10 @@
 
     near_half = zh == 0
     pl.when(near_half)(pass_up)
+
+    for q in range(1, SUBS):
+        for k in (1, 2, 3):
+            cot_copy(q, k).start()
 
     mine = pl.ds(pl.multiple_of(c * 128, 128), 128)
     other = pl.ds(pl.multiple_of((1 - c) * 128, 128), 128)
@@ -372,7 +376,7 @@
 
     def unit(k, u):
         way = jnp.where(k == 0, inner, 1 - inner)
-        v = jnp.where(k == 0, u, u - (36 - 8 * depth))
+        v = jnp.where(k == 0, u, u - (36 - 10 * depth))
 
         @pl.when((v >= 0) & (v < jnp.where(k == 0, count_in, count_out)))
         def _():
@@ -546,8 +550,21 @@
 
 
 def copy_kernel(*refs):
-    for a, b in zip(refs[:3], refs[3:]):
-        b[...] = a[...]
+    ins, outs, held, sem_in, sem_out = refs[:3], refs[3:6], refs[6:9], refs[9], refs[10]
+    pieces = [(0, pl.ds(i * 64, 64)) for i in range(4)] + [(1, pl.ds(0, 64)), (2, pl.ds(0, 64))]
+    fetch = [
+        pltpu.make_async_copy(ins[n].at[at], held[n].at[at], sem_in.at[i]) for i, (n, at) in enumerate(pieces)
+    ]
+    write = [
+        pltpu.make_async_copy(held[n].at[at], outs[n].at[at], sem_out.at[i]) for i, (n, at) in enumerate(pieces)
+    ]
+    for copy in fetch:
+        copy.start()
+    for a, b in zip(fetch, write):
+        a.wait()
+        b.start()
+    for copy in write:
+        copy.wait()
 
 
 def on_device(tokens, norm_gain, cotangent, layer_weight, shared_copy, master, momentum):
@@ -594,8 +611,9 @@
     layer_next, master_next, momentum_next = pl.pallas_call(
         copy_kernel,
         out_shape=[jax.ShapeDtypeStruct(r.shape, r.dtype) for r in results],
-        in_specs=[pl.BlockSpec(memory_space=vmem)] * 3,
-        out_specs=[pl.BlockSpec(memory_space=vmem)] * 3,
+        in_specs=[pl.BlockSpec(memory_space=hbm)] * 3,
+        out_specs=[pl.BlockSpec(memory_space=hbm)] * 3,
+        scratch_shapes=[vmem(r.shape, r.dtype) for r in results] + [dma((6,)), dma((6,))],
         name="write_out",
         compiler_params=pltpu.CompilerParams(vmem_limit_bytes=60 << 20),
     )(*results)

time: 100 us -> 100 us (level)
  the two profiles are of different devices: /device:TPU:160 before, /device:TPU:166 now
where the time goes in v4:
time: 100 us; the launch traced here: 99.8 us
  Pallas kernels  99.1 us (99%)
    pallas_call x1, Pallas kernels, on_device(): pl.pallas_call(kernel, out_shape=[jax.ShapeDtypeStruct((256, 1024), BF16)...  97.2 us

profile of v4, /device:TPU:166, one launch (start us, length us, event | category | flops | bytes accessed | tf_op | source)
XLA Modules:
  0.0 99.8 jit_solution(16769853369791330512)
XLA Ops:
  0.6 97.2 %diloco_step.1 = (bf16[256,1024]{1,0:T(8,128)(2,1)}, f32[64,256]{1,0:T(8,128)}, f32[64,256]{1,0:T(8,128)}) custom-call(bf16[128,8192]{1,0:T(8,128)(2,1)} %bitcast.9, bf16[64,128]{1,0:T(8,128)(2,1)} %bitcast.17, bf16[128,1024]{1,0:T(8,128)(2,1)} %bitcast.12, bf16[256,1024]{1,0:T(8,128)(2,1)} %bitcast.10, bf16[256,1024]{1,0:T(8,128)(2,1)} %shared_hbm.1, ...), custom_call_target="tpu_custom_call" | custom-call | flops 2147483648 | bytes 5242880 | tf_op jit(solution)/shard_map/diloco_step/pallas_call | solution.py:591
  97.9 1.9 %write_out.1 = (bf16[256,1024]{1,0:T(8,128)(2,1)}, f32[64,256]{1,0:T(8,128)}, f32[64,256]{1,0:T(8,128)}) custom-call(bf16[256,1024]{1,0:T(8,128)(2,1)} %get-tuple-element.9.refs_0_, f32[64,256]{1,0:T(8,128)} %get-tuple-element.10.refs_1_, f32[64,256]{1,0:T(8,128)} %get-tuple-element.11.refs_2_), custom_call_target="tpu_custom_call" | custom-call | tf_op jit(solution)/shard_map/write_out/pallas_call | solution.py:611

commit v5 on v4

--- a/solution.py
+++ b/solution.py
@@ -356,7 +356,8 @@
 
     def stream(way, v):
         s, j = v // PARTS, lax.rem(v, PARTS)
-        to = jnp.where(way == 0, z + 1, z - 1)
+        up = ((way == 0) & (z < NZ - 1)) | (z == 0)
+        to = jnp.where(up, z + 1, z - 1)
         slot = jnp.where(way == 0, v, NZ * PARTS + PARTS - 1 - v)
         return remote(
             buf.at[way, s, j], buf.at[way, s, j], su.at[way, lax.rem(v, DEPTH)], ru.at[slot], device(z=to)

time: 100 us -> 100 us (level)
  the two profiles are of different devices: /device:TPU:166 before, /device:TPU:162 now
where the time goes in v5:
time: 100 us; the launch traced here: 99.8 us
  Pallas kernels  99.1 us (99%)
    pallas_call x1, Pallas kernels, on_device(): pl.pallas_call(kernel, out_shape=[jax.ShapeDtypeStruct((256, 1024), BF16)...  97.2 us

profile of v5, /device:TPU:162, one launch (start us, length us, event | category | flops | bytes accessed | tf_op | source)
XLA Modules:
  0.0 99.8 jit_solution(14599194719982089316)
XLA Ops:
  0.6 97.2 %diloco_step.1 = (bf16[256,1024]{1,0:T(8,128)(2,1)}, f32[64,256]{1,0:T(8,128)}, f32[64,256]{1,0:T(8,128)}) custom-call(bf16[128,8192]{1,0:T(8,128)(2,1)} %bitcast.9, bf16[64,128]{1,0:T(8,128)(2,1)} %bitcast.17, bf16[128,1024]{1,0:T(8,128)(2,1)} %bitcast.12, bf16[256,1024]{1,0:T(8,128)(2,1)} %bitcast.10, bf16[256,1024]{1,0:T(8,128)(2,1)} %shared_hbm.1, ...), custom_call_target="tpu_custom_call" | custom-call | flops 2147483648 | bytes 5242880 | tf_op jit(solution)/shard_map/diloco_step/pallas_call | solution.py:592
  97.9 1.9 %write_out.1 = (bf16[256,1024]{1,0:T(8,128)(2,1)}, f32[64,256]{1,0:T(8,128)}, f32[64,256]{1,0:T(8,128)}) custom-call(bf16[256,1024]{1,0:T(8,128)(2,1)} %get-tuple-element.9.refs_0_, f32[64,256]{1,0:T(8,128)} %get-tuple-element.10.refs_1_, f32[64,256]{1,0:T(8,128)} %get-tuple-element.11.refs_2_), custom_call_target="tpu_custom_call" | custom-call | tf_op jit(solution)/shard_map/write_out/pallas_call | solution.py:612
